TPU v7x, 32 devices: a whole 2x2x4 slice. The times are simulated.
32 devices in a mesh: groups: 2 (over y), lon: 4 (over x, core), lat: 4 (over z).
Axes of the slice: x: 2, y: 2, z: 4, core: 2. Of those that a mesh axis runs over, the one named last changes fastest.
Arguments:
- node_latent: bfloat16 [16384, 512], P(('groups', 'lon', 'lat')), parts along dimension 0, may hold values from -6 to 6
- fine_edges: bfloat16 [98304, 512], P(('groups', 'lon', 'lat')), parts along dimension 0, may hold values from -6 to 6
- coarse_edges: bfloat16 [32768, 512], P(('groups', 'lon', 'lat')), parts along dimension 0, may hold values from -6 to 6
- fine_sender: int32 [98304], P(('groups', 'lon', 'lat')), parts along dimension 0, may hold values from 0 to 8191, as said below
- fine_receiver: int32 [98304], P(('groups', 'lon', 'lat')), parts along dimension 0, may hold values from 0 to 511
- coarse_peer: int32 [32768, 1], P(('groups', 'lon', 'lat')), parts along dimension 0, may hold values from 0 to 15; in each aligned block of 1024 rows (0 to 1023, 1024 to 2047, ...) at most 128 rows name the same one
- coarse_row: int32 [32768], P(('groups', 'lon', 'lat')), parts along dimension 0, may hold values from 0 to 127
- coarse_receiver: int32 [32768], P(('groups', 'lon', 'lat')), parts along dimension 0, may hold values from 0 to 511
- edge_in: bfloat16 [1536, 512], replicated, may hold values from -0.15625 to 0.15625
- edge_out: bfloat16 [512, 512], replicated, may hold values from -0.25 to 0.25
- edge_gain: float32 [512], replicated, may hold values from 0.1 to 1.9
- node_in: bfloat16 [1024, 512], replicated, may hold values from -0.1875 to 0.1875
- node_out: bfloat16 [512, 512], replicated, may hold values from -0.25 to 0.25
- node_gain: float32 [512], replicated, may hold values from 0.1 to 1.9
Outputs:
- node_next: bfloat16 [16384, 512], P(('groups', 'lon', 'lat')), parts along dimension 0
- fine_next: bfloat16 [98304, 512], P(('groups', 'lon', 'lat')), parts along dimension 0
- coarse_next: bfloat16 [32768, 512], P(('groups', 'lon', 'lat')), parts along dimension 0
There are 2 independent parts, one for each index of `groups`. A program takes and returns all parts, laid end to end along the dimension named above; an argument that names none is the same for every part. Nothing has to cross between parts.
Inputs may be any that keep to these rules, and one draw needn't show every extreme that they name: `fine_sender`: A partition's row r lies at grid place (r // 16, r % 16) of a 32 x 16 local grid, the first coordinate along longitude. The sender of a finest-level edge lies in the edge's own partition or in one of the eight partitions beside it: longitude sector one lower, equal or one higher (sectors wrap around), latitude band one lower, equal or one higher (bands do not wrap); partition index = sector index * number of bands + band index. A sender in the sector one lower has first coordinate 32 - 1, in the sector one higher first coordinate 0; a sender in the band one lower has second coordinate 16 - 1, in the band one higher second coordinate 0. `coarse_peer`: among the 1024 coarser-level edges of one partition, at most 128 name the same sender partition.
All inputs are finite; a program needn't handle non-finite values.
Results may differ from a plain program's by a relative error of at most 0.0053.
Values may be sent and summed in bfloat16 or wider, within the bound.
A program may use at most 128 MiB of HBM per device.

v0:
```python
import jax
import jax.numpy as jnp
from jax import lax
from jax.sharding import PartitionSpec as P

GRID_LAT = 16


def with_halo(cells, sides, width, closed):
    for axis, dim in sides:
        count = lax.axis_size(axis)
        ends = count if closed else count - 1
        head = lax.slice_in_dim(cells, 0, width, axis=dim)
        tail = lax.slice_in_dim(cells, cells.shape[dim] - width, cells.shape[dim], axis=dim)
        cells = jnp.concatenate(
            [
                lax.ppermute(tail, axis, [(i, (i + 1) % count) for i in range(ends)]),
                cells,
                lax.ppermute(head, axis, [((i + 1) % count, i) for i in range(ends)]),
            ],
            axis=dim,
        )
    return cells


def layer_norm(values, gain):
    mean = jnp.mean(values, axis=-1, keepdims=True)
    centred = values - mean
    scale = lax.rsqrt(jnp.mean(centred * centred, axis=-1, keepdims=True) + 1e-05)
    return centred * scale * gain


def select_rows(table, picks):
    picker = (picks[:, None] == jnp.arange(table.shape[0], dtype=jnp.int32)[None, :]).astype(
        jnp.bfloat16
    )
    return jnp.dot(picker, table, preferred_element_type=jnp.float32).astype(jnp.bfloat16)


def shards(
    node_latent,
    fine_edges,
    coarse_edges,
    fine_sender,
    fine_receiver,
    coarse_peer,
    coarse_row,
    coarse_receiver,
    edge_in,
    edge_out,
    edge_gain,
    node_in,
    node_out,
    node_gain,
):
    node_count = node_latent.shape[0]
    width = node_latent.shape[1]
    coarse_count = node_count // 4
    fine_count = fine_edges.shape[0]
    lon_size = lax.axis_size("lon")
    lat_size = lax.axis_size("lat")
    lon_here = lax.axis_index("lon")
    lat_here = lax.axis_index("lat")
    grid_lon = node_count // GRID_LAT
    block = node_latent.reshape(grid_lon, GRID_LAT, width)
    sectors = with_halo(block, (("lon", 0),), 1, True)
    square = with_halo(sectors, (("lat", 1),), 1, False)
    beside_all = square.reshape((grid_lon + 2) * (GRID_LAT + 2), width)
    source = fine_sender // node_count
    row_index = fine_sender % node_count
    lon_shift = (source // lat_size - lon_here + 1 + lon_size) % lon_size - 1
    lat_shift = source % lat_size - lat_here
    place_i = row_index // GRID_LAT + 1 + lon_shift * grid_lon
    place_j = row_index % GRID_LAT + 1 + lat_shift * GRID_LAT
    local_sender = place_i * (GRID_LAT + 2) + place_j
    near = select_rows(beside_all, local_sender)
    peers = coarse_peer[:, 0]
    everyone = lax.all_gather(node_latent[:coarse_count], ("lon", "lat"), axis=0, tiled=True)
    far = jnp.take(everyone, peers * coarse_count + coarse_row, axis=0)
    targets = jnp.concatenate([fine_receiver, coarse_receiver], axis=0)
    edges = jnp.concatenate([fine_edges, coarse_edges], axis=0)
    senders = jnp.concatenate([near, far], axis=0)
    receivers = select_rows(node_latent, targets)
    joined = jnp.concatenate([edges, senders, receivers], axis=1)
    edge_hidden = jax.nn.silu(jnp.dot(joined, edge_in, preferred_element_type=jnp.float32)).astype(
        jnp.bfloat16
    )
    edge_change = layer_norm(
        jnp.dot(edge_hidden, edge_out, preferred_element_type=jnp.float32), edge_gain
    )
    message = edge_change.astype(jnp.bfloat16)
    edge_next = (edges.astype(jnp.float32) + edge_change).astype(jnp.bfloat16)
    selector = (jnp.arange(node_count, dtype=jnp.int32)[:, None] == targets[None, :]).astype(
        jnp.bfloat16
    )
    gathered = jnp.dot(selector, message, preferred_element_type=jnp.float32).astype(jnp.bfloat16)
    node_joined = jnp.concatenate([node_latent, gathered], axis=1)
    node_hidden = jax.nn.silu(
        jnp.dot(node_joined, node_in, preferred_element_type=jnp.float32)
    ).astype(jnp.bfloat16)
    node_change = layer_norm(
        jnp.dot(node_hidden, node_out, preferred_element_type=jnp.float32), node_gain
    )
    node_next = (node_latent.astype(jnp.float32) + node_change).astype(jnp.bfloat16)
    return (node_next, edge_next[:fine_count], edge_next[fine_count:])


def solution(mesh):
    return jax.shard_map(
        shards,
        mesh=mesh,
        in_specs=(
            P(("groups", "lon", "lat"), None),
            P(("groups", "lon", "lat"), None),
            P(("groups", "lon", "lat"), None),
            P(("groups", "lon", "lat")),
            P(("groups", "lon", "lat")),
            P(("groups", "lon", "lat"), None),
            P(("groups", "lon", "lat")),
            P(("groups", "lon", "lat")),
            P(),
            P(),
            P(),
            P(),
            P(),
            P(),
        ),
        out_specs=(
            P(("groups", "lon", "lat"), None),
            P(("groups", "lon", "lat"), None),
            P(("groups", "lon", "lat"), None),
        ),
        check_vma=False,
    )
```

profile of v0, /device:TPU:0, one launch (start us, length us, event | category | flops | bytes accessed | tf_op | source)
XLA Modules:
  0.0 120.4 jit_solution(429038227119707170)
XLA Ops:
  7.2 0.0 copy-start
  7.2 0.0 copy-start.3
  7.2 0.0 copy-start.4
  7.2 0.0 all-gather.2.cloned.1.call-start
  7.2 1.7 %slice.33 = bf16[128,512]{1,0:T(8,128)(2,1)} slice(bf16[512,512]{1,0:T(8,128)(2,1)} %param.14), slice={[0:128], [0:512]} | slice | bytes 262144 | tf_op jit(solution)/shard_map/slice | solution.py:78
  8.9 0.0 all-gather.2.cloned.1.call-update
  9.0 0.7 slice_bitcast_fusion.1
  9.7 0.5 collective-permute-start
  10.2 1.9 %collective-permute-start.1 = (bf16[1,16,512]{2,1,0:T(8,128)(2,1)S(1)}, bf16[1,16,512]{2,1,0:T(8,128)(2,1)S(1)}, u32[]{:S(2)}, u32[]{:S(2)}) collective-permute-start(bf16[1,16,512]{2,1,0:T(8,128)(2,1)S(1)} %get-tuple-element.12), channel_id=1, source_target_pairs={{4,0},{8,4},{12,8},{0,12},{5,1},{9,5},{13,9},{1,13},{6,2},{10,6},{... | collective-permute-start | bytes 49160 | tf_op jit(solution)/shard_map/ppermute | solution.py:19
  12.1 0.7 constant_dynamic-update-slice_fusion.1
  12.8 0.7 constant_dynamic-update-slice_fusion
  13.5 0.7 broadcast_multiply_fusion.1
  14.2 0.8 fusion.44
  14.9 5.4 %fusion.14 = bf16[4096,512]{0,1:T(8,128)(2,1)} fusion(bf16[512,512]{1,0:T(8,128)(2,1)} %param.14, s32[4096]{0:T(1024)S(1)} %constant_dynamic-update-slice_fusion), kind=kOutput, calls=%fused_computation.22 | convolution fusion | flops 2151677952 | bytes 4734976 | tf_op jit(solution)/shard_map/dot_general | solution.py:37
  20.4 0.0 copy-done.4
  20.4 0.0 collective-permute-done
  20.4 0.0 collective-permute-done.1
  20.4 0.0 copy-done.3
  20.4 0.1 pad_maximum_fusion.3
  20.5 4.3 %collective-permute-start.2 = (bf16[34,1,512]{2,1,0:T(2,128)(2,1)S(1)}, bf16[34,1,512]{2,1,0:T(2,128)(2,1)S(1)}, u32[]{:S(2)}, u32[]{:S(2)}) collective-permute-start(bf16[34,1,512]{2,1,0:T(2,128)(2,1)S(1)} %get-tuple-element.9), channel_id=1, source_target_pairs={{0,1},{1,2},{2,3},{4,5},{5,6},{6,7},{8,9},{9,10},{10,11},{12,13},{... | collective-permute-start | bytes 104456 | tf_op jit(solution)/shard_map/ppermute | solution.py:17
  24.8 1.5 %collective-permute-start.3 = (bf16[34,1,512]{2,1,0:T(2,128)(2,1)S(1)}, bf16[34,1,512]{2,1,0:T(2,128)(2,1)S(1)}, u32[]{:S(2)}, u32[]{:S(2)}) collective-permute-start(bf16[34,1,512]{2,1,0:T(2,128)(2,1)S(1)} %get-tuple-element.10), channel_id=1, source_target_pairs={{1,0},{2,1},{3,2},{5,4},{6,5},{7,6},{9,8},{10,9},{11,10},{13,12},{... | collective-permute-start | bytes 104456 | tf_op jit(solution)/shard_map/ppermute | solution.py:19
  26.3 1.0 copy.24
  27.3 4.7 %copy.25 = bf16[3072,512]{0,1:T(8,128)(2,1)} copy(bf16[3072,512]{1,0:T(8,128)(2,1)} %param.15) | data formatting | bytes 6291456 | tf_op args[1]
  32.0 1.5 %copy.26 = bf16[1024,512]{0,1:T(8,128)(2,1)S(1)} copy(bf16[1024,512]{1,0:T(8,128)(2,1)} %param.16) | data formatting | bytes 2097152 | tf_op args[2]
  33.5 0.0 collective-permute-done.2
  33.5 0.0 collective-permute-done.3
  33.6 1.3 %pad_maximum_fusion = bf16[34,18,512]{2,1,0:T(8,128)(2,1)} fusion(bf16[34,1,512]{2,1,0:T(2,128)(2,1)S(1)} %collective-permute-done.3, bf16[1,16,512]{2,1,0:T(8,128)(2,1)S(1)} %collective-permute-done.1, bf16[32,16,512]{2,1,0:T(8,128)(2,1)S(1)} %bitcast.13, bf16[1,16,512]{2,1,0:T(8,128)(2,1)S(1)} %collective-permute-done, ...), kind=kLoop, calls=%fused_computation.41 | loop fusion | flops 3133440 | bytes 1253376 | tf_op jit(solution)/shard_map/concatenate | solution.py:15
  34.9 2.1 %reshape.51 = bf16[612,512]{1,0:T(8,128)(2,1)} reshape(bf16[34,18,512]{2,1,0:T(8,128)(2,1)} %pad_maximum_fusion) | data formatting | bytes 1253376 | tf_op jit(solution)/shard_map/reshape | solution.py:68
  37.0 6.0 %fusion.15 = bf16[3072,512]{0,1:T(8,128)(2,1)} fusion(bf16[612,512]{1,0:T(8,128)(2,1)} %reshape.51, s32[3072]{0:T(1024)S(1)} %fusion.44), kind=kOutput, calls=%fused_computation.23 | convolution fusion | flops 1928638464 | bytes 3784704 | tf_op jit(solution)/shard_map/dot_general | solution.py:37
  43.0 11.6 %all-gather.2.cloned.1.call-done = bf16[2048,512]{1,0:T(8,128)(2,1)} async-done(((bf16[128,512]{1,0:T(8,128)(2,1)}), bf16[2048,512]{1,0:T(8,128)(2,1)}) %all-gather.2.cloned.1.call-update) | async-done | bytes 2097168 | tf_op jit(solution)/shard_map/all_gather | solution.py:78
  54.6 7.0 %gather_fusion = bf16[1024,512]{1,0:T(8,128)(2,1)} fusion(bf16[2048,512]{1,0:T(8,128)(2,1)} %all-gather.2.cloned.1.call-done, s32[1024]{0:T(1024)S(1)} %broadcast_clamp_fusion), kind=kCustom, calls=%fused_computation | custom fusion | bytes 2101248 | tf_op jit(solution)/shard_map/jit(_take)/gather | solution.py:79
  61.6 2.3 %copy.27 = bf16[1024,512]{0,1:T(8,128)(2,1)} copy(bf16[1024,512]{1,0:T(8,128)(2,1)} %gather_fusion) | data formatting | bytes 2097152 | tf_op jit(solution)/shard_map/jit(_take)/gather | solution.py:79
  63.9 2.3 %broadcast_select_fusion = bf16[1024,512]{0,1:T(8,128)(2,1)} fusion(bf16[1024,512]{0,1:T(8,128)(2,1)} %copy.27, pred[1024]{0:T(1024)(128)(4,1)S(1)} %compare_and_fusion), kind=kLoop, calls=%fused_computation.39 | loop fusion | flops 524288 | bytes 2098176 | tf_op jit(solution)/shard_map/jit(_take)/select_n | solution.py:79
  66.1 0.0 copy-done
  66.2 20.3 %fusion.67 = (f32[4096]{0:T(1024)S(1)}, f32[4096,512]{0,1:T(8,128)}) fusion(bf16[512,512]{1,0:T(8,128)(2,1)} %param.23, bf16[1536,512]{1,0:T(8,128)(2,1)S(1)} %copy-done, bf16[4096,512]{0,1:T(8,128)(2,1)} %fusion.14, bf16[1024,512]{0,1:T(8,128)(2,1)} %broadcast_select_fusion, bf16[3072,512]{0,1:T(8,128)(2,1)} %fusion.15, bf16[1024,512]{0,1:T(8,128)(2,1)S(1)} %copy.26, ...), kind=kOutput, calls=%fused_computation.103 | convolution fusion | flops 8665427968 | bytes 23085056 | tf_op jit(solution)/shard_map/dot_general | solution.py:89
  86.5 0.0 copy-start.1
  86.5 0.0 copy-start.5
  86.5 4.5 %multiply_reduce_fusion = f32[4096]{0:T(1024)S(1)} fusion(f32[4096,512]{0,1:T(8,128)} %get-tuple-element.14, f32[4096]{0:T(1024)S(1)} %broadcast_multiply_fusion), kind=kLoop, calls=%fused_computation.13 | loop fusion | flops 6287360 | bytes 8421376 | tf_op jit(solution)/shard_map/reduce_sum | solution.py:29
  91.0 1.2 %copy-done.1 = f32[4096,512]{0,1:T(8,128)S(1)} copy-done((f32[4096,512]{0,1:T(8,128)S(1)}, f32[4096,512]{0,1:T(8,128)}, u32[]{:S(2)}) %copy-start.1) | copy-done | bytes 8388632
  92.3 0.0 copy-done.5
  92.3 3.7 %add_convert_fusion = bf16[4096,512]{0,1:T(8,128)(2,1)S(1)} fusion(f32[4096,512]{0,1:T(8,128)S(1)} %copy-done.1, bf16[1024,512]{0,1:T(8,128)(2,1)S(1)} %copy.26, bf16[3072,512]{0,1:T(8,128)(2,1)} %copy.25, f32[512]{0:T(512)S(1)} %copy-done.5, f32[4096]{0:T(1024)S(1)} %add_rsqrt_fusion, f32[4096]{0:T(1024)S(1)} %broadcast_multiply_fusion), kind=kLoop, calls=%fused_computation.11 | loop fusion | flops 18874368 | bytes 16812032 | tf_op jit(solution)/shard_map/convert_element_type | solution.py:92
  96.0 0.0 copy-start.2
  96.0 2.1 %slice.38 = bf16[3072,512]{0,1:T(8,128)(2,1)} slice(bf16[4096,512]{0,1:T(8,128)(2,1)S(1)} %add_convert_fusion), slice={[0:3072], [0:512]} | slice | bytes 6291456 | tf_op jit(solution)/shard_map/slice | solution.py:105
  98.2 0.7 copy-done.2
  98.9 0.0 slice-start
  98.9 3.4 %fusion.28 = bf16[512,512]{1,0:T(8,128)(2,1)} fusion(f32[4096,512]{0,1:T(8,128)S(1)} %copy-done.1, f32[512]{0:T(512)S(1)} %copy-done.5, f32[4096]{0:T(1024)S(1)} %add_rsqrt_fusion, f32[4096]{0:T(1024)S(1)} %broadcast_multiply_fusion, s32[4096]{0:T(1024)S(1)} %constant_dynamic-update-slice_fusion), kind=kOutput, calls=%fused_computation.31 | convolution fusion | flops 2158231552 | bytes 8964096 | tf_op jit(solution)/shard_map/dot_general | solution.py:96
  102.4 0.0 copy-start.6
  102.4 4.7 %copy.29 = bf16[3072,512]{1,0:T(8,128)(2,1)} copy(bf16[3072,512]{0,1:T(8,128)(2,1)} %slice.38) | data formatting | bytes 6291456
  107.0 0.0 slice-done
  107.0 1.3 %copy.30 = bf16[1024,512]{1,0:T(8,128)(2,1)} copy(bf16[1024,512]{0,1:T(8,128)(2,1)S(1)} %slice-done) | data formatting | bytes 2097152
  108.3 2.8 %fusion.70 = (f32[512]{0:T(512)S(1)}, f32[512,512]{0,1:T(8,128)S(1)}) fusion(bf16[512,512]{1,0:T(8,128)(2,1)} %param.26, bf16[1024,512]{1,0:T(8,128)(2,1)} %param.25, bf16[512,512]{1,0:T(8,128)(2,1)} %fusion.28, bf16[512,512]{1,0:T(8,128)(2,1)S(1)} %copy-done.3), kind=kOutput, calls=%fused_computation.104 | convolution fusion | flops 808975872 | bytes 3672064 | tf_op jit(solution)/shard_map/dot_general | solution.py:102
  111.1 0.2 multiply_reduce_fusion.1
  111.3 0.0 copy-done.6
  111.3 1.3 %add_convert_fusion.1 = bf16[512,512]{0,1:T(8,128)(2,1)S(1)} fusion(bf16[512,512]{0,1:T(8,128)(2,1)} %copy.24, f32[512,512]{0,1:T(8,128)S(1)} %get-tuple-element.16, f32[512]{0:T(512)S(1)} %copy-done.6, f32[512]{0:T(512)S(1)} %add_rsqrt_fusion.1, f32[512]{0:T(512)S(1)} %broadcast_multiply_fusion.2), kind=kLoop, calls=%fused_computation.36 | loop fusion | flops 1572864 | bytes 2103296 | tf_op jit(solution)/shard_map/convert_element_type | solution.py:104
  112.6 1.0 copy.28
  (6 shorter events, 0.0 us)
Async XLA Ops:
  7.2 59.0 %copy-start = (bf16[1536,512]{1,0:T(8,128)(2,1)S(1)}, bf16[1536,512]{1,0:T(8,128)(2,1)}, u32[]{:S(2)}) copy-start(bf16[1536,512]{1,0:T(8,128)(2,1)} %param.22) | copy-start | bytes 4718596
  7.2 13.2 %copy-start.3 = (bf16[512,512]{1,0:T(8,128)(2,1)S(1)}, bf16[512,512]{1,0:T(8,128)(2,1)}, u32[]{:S(2)}) copy-start(bf16[512,512]{1,0:T(8,128)(2,1)} %param.14) | copy-start | bytes 1572868
  7.2 13.2 %copy-start.4 = (s32[1024]{0:T(1024)S(1)}, s32[1024]{0:T(1024)}, u32[]{:S(2)}) copy-start(s32[1024]{0:T(1024)} %param.20) | copy-start | bytes 12292
  7.2 47.4 %all-gather.2.cloned.1.call-start = ((), (), s32[]{:S(2)}) async-start(), calls=%async_computation | async-start | bytes 2228224 | tf_op jit(solution)/shard_map/all_gather | solution.py:78
  9.7 10.7 %collective-permute-start = (bf16[1,16,512]{2,1,0:T(8,128)(2,1)S(1)}, bf16[1,16,512]{2,1,0:T(8,128)(2,1)S(1)}, u32[]{:S(2)}, u32[]{:S(2)}) collective-permute-start(bf16[1,16,512]{2,1,0:T(8,128)(2,1)S(1)} %get-tuple-element.11), channel_id=1, source_target_pairs={{0,4},{4,8},{8,12},{12,0},{1,5},{5,9},{9,13},{13,1},{2,6},{6,10},{... | collective-permute-start | bytes 49160 | tf_op jit(solution)/shard_map/ppermute | solution.py:17
  10.2 10.2 %collective-permute-start.1 = (bf16[1,16,512]{2,1,0:T(8,128)(2,1)S(1)}, bf16[1,16,512]{2,1,0:T(8,128)(2,1)S(1)}, u32[]{:S(2)}, u32[]{:S(2)}) collective-permute-start(bf16[1,16,512]{2,1,0:T(8,128)(2,1)S(1)} %get-tuple-element.12), channel_id=1, source_target_pairs={{4,0},{8,4},{12,8},{0,12},{5,1},{9,5},{13,9},{1,13},{6,2},{10,6},{... | collective-permute-start | bytes 49160 | tf_op jit(solution)/shard_map/ppermute | solution.py:19
  20.5 13.0 %collective-permute-start.2 = (bf16[34,1,512]{2,1,0:T(2,128)(2,1)S(1)}, bf16[34,1,512]{2,1,0:T(2,128)(2,1)S(1)}, u32[]{:S(2)}, u32[]{:S(2)}) collective-permute-start(bf16[34,1,512]{2,1,0:T(2,128)(2,1)S(1)} %get-tuple-element.9), channel_id=1, source_target_pairs={{0,1},{1,2},{2,3},{4,5},{5,6},{6,7},{8,9},{9,10},{10,11},{12,13},{... | collective-permute-start | bytes 104456 | tf_op jit(solution)/shard_map/ppermute | solution.py:17
  24.8 8.7 %collective-permute-start.3 = (bf16[34,1,512]{2,1,0:T(2,128)(2,1)S(1)}, bf16[34,1,512]{2,1,0:T(2,128)(2,1)S(1)}, u32[]{:S(2)}, u32[]{:S(2)}) collective-permute-start(bf16[34,1,512]{2,1,0:T(2,128)(2,1)S(1)} %get-tuple-element.10), channel_id=1, source_target_pairs={{1,0},{2,1},{3,2},{5,4},{6,5},{7,6},{9,8},{10,9},{11,10},{13,12},{... | collective-permute-start | bytes 104456 | tf_op jit(solution)/shard_map/ppermute | solution.py:19
  86.5 5.8 %copy-start.1 = (f32[4096,512]{0,1:T(8,128)S(1)}, f32[4096,512]{0,1:T(8,128)}, u32[]{:S(2)}) copy-start(f32[4096,512]{0,1:T(8,128)} %get-tuple-element.14) | copy-start | bytes 25165828
  86.5 5.8 %copy-start.5 = (f32[512]{0:T(512)S(1)}, f32[512]{0:T(512)}, u32[]{:S(2)}) copy-start(f32[512]{0:T(512)} %param.24) | copy-start | bytes 6148
  96.0 2.9 %copy-start.2 = (bf16[4096,512]{0,1:T(8,128)(2,1)}, bf16[4096,512]{0,1:T(8,128)(2,1)S(1)}, u32[]{:S(2)}) copy-start(bf16[4096,512]{0,1:T(8,128)(2,1)S(1)} %add_convert_fusion) | copy-start | bytes 12582916
  98.9 8.1 %slice-start = ((bf16[4096,512]{0,1:T(8,128)(2,1)}), bf16[1024,512]{0,1:T(8,128)(2,1)S(1)}, s32[]{:S(2)}) async-start(bf16[4096,512]{0,1:T(8,128)(2,1)} %copy-done.2), calls=%async_computation.1 | async-start | bytes 2097152 | tf_op jit(solution)/shard_map/slice | solution.py:105
  102.4 9.0 %copy-start.6 = (f32[512]{0:T(512)S(1)}, f32[512]{0:T(512)}, u32[]{:S(2)}) copy-start(f32[512]{0:T(512)} %param.27) | copy-start | bytes 6148
Sparse Core Ops, SparseCore 0:
  10.2 44.3 all-gather.1
where the time goes:
time: 121 us; the launch traced here: 120 us
  matrix products  38 us (31%)
  local copies, waits for them, and re-layouts  33.5 us (28%)
  other arithmetic  14.9 us (12%)
  between operations  14.2 us (12%)
  waiting for transfers between devices  11.6 us (10%)
  starting transfers between devices  8.19 us (7%)
    dot_general x1, matrix products, shards(): jnp.dot(edge_hidden, edge_out, preferred_element_type=jnp.float32)  20.3 us
    unnamed x21, local copies, waits for them, and re-layouts  16.9 us
    all_gather x1, waiting for transfers between devices, shards(): lax.all_gather(node_latent[:coarse_count], ('lon', 'lat'), axis=0, tiled=...  11.6 us
    dot_general x2, matrix products, select_rows(): jnp.dot(picker, table, preferred_element_type=jnp.float32)  11.4 us
    gather x2, local copies, waits for them, and re-layouts, shards(): far = jnp.take(everyone, peers * coarse_count + coarse_row, axis=0)  9.24 us
    ppermute x2, starting transfers between devices, with_halo(): lax.ppermute(tail, axis, [(i, (i + 1) % count) for i in range(ends)])  4.75 us
    reduce_sum x2, other arithmetic, layer_norm(): jnp.mean(centred * centred, axis=-1, keepdims=True) + 1e-05  4.69 us
    convert_element_type x1, other arithmetic, shards(): edge_next = (edges.astype(jnp.float32) + edge_change).astype(jnp.bfloat16)  3.74 us
  transfers between devices with their start and end apart: 5, of which 1 were waited for; matrix products, arithmetic and copies ran while one was open for 21% of the time, Pallas kernels for 0%

commit v1 on v0

--- a/solution.py
+++ b/solution.py
@@ -1,9 +1,480 @@
 import jax
 import jax.numpy as jnp
 from jax import lax
+from jax.experimental import pallas as pl
+from jax.experimental.pallas import tpu as pltpu
 from jax.sharding import PartitionSpec as P
 
 GRID_LAT = 16
+MESH = pl.DeviceIdType.MESH
+GROUP = 128
+TILE = 512
+SUB = 256
+RIM_LON = 16
+RIM_LAT = 32
+HALO = 256
+
+
+def one_hot(rows, width):
+    lanes = lax.broadcasted_iota(jnp.int32, (GROUP, GROUP), 1).astype(jnp.float32)
+    tall = []
+    for row in rows:
+        column = jnp.transpose(jnp.broadcast_to(row, (GROUP, GROUP)))
+        tall.append(
+            jnp.concatenate(
+                [
+                    jnp.where(column == lanes + float(first), 1.0, 0.0).astype(jnp.bfloat16)
+                    for first in range(0, width, GROUP)
+                ],
+                axis=1,
+            )
+        )
+    return jnp.concatenate(tall, axis=0)
+
+
+def one_hot_across(rows, height):
+    places = lax.broadcasted_iota(jnp.int32, (height, GROUP), 0).astype(jnp.float32)
+    return jnp.concatenate(
+        [jnp.where(places == row, 1.0, 0.0).astype(jnp.bfloat16) for row in rows], axis=1
+    )
+
+
+def matmul(a, b):
+    return jnp.dot(a, b, preferred_element_type=jnp.float32)
+
+
+def silu_of_twice(half):
+    return (half * (1.0 + jnp.tanh(half))).astype(jnp.bfloat16)
+
+
+def normed(values, gain):
+    scale = 1.0 / values.shape[-1]
+    mean = jnp.sum(values, axis=-1, keepdims=True) * scale
+    centred = values - mean
+    square = jnp.sum(centred * centred, axis=-1, keepdims=True) * scale
+    return centred * lax.rsqrt(square + 1e-05) * gain
+
+
+def fine_kernel(
+    node_ref,
+    edges_ref,
+    sender_ref,
+    receiver_ref,
+    edge_in_ref,
+    edge_out_ref,
+    gain_ref,
+    message_ref,
+    total_ref,
+    every_ref,
+    recv_table_ref,
+    table,
+    rims,
+    edge_half,
+    edge_buf,
+    message_buf,
+    sender_ids,
+    receiver_ids,
+    edge_sem,
+    message_sem,
+    own_sem,
+    halo_send,
+    halo_recv,
+    send_sem,
+    recv_sem,
+):
+    nodes, width = node_ref.shape
+    tiles = edges_ref.shape[0] // TILE
+    lat_size = lax.axis_size("lat")
+    lon = lax.axis_index("lon")
+    lat = lax.axis_index("lat")
+    twin = lon + 1 - 2 * lax.rem(lon, 2)
+    across = lax.rem(lon + 2, 4)
+    bands = [
+        lat,
+        lat + 1 - 2 * lax.rem(lat, 2),
+        lax.rem(lat + 2, 4),
+        3 - lat,
+    ]
+    lon_up, lon_down = lax.rem(lon + 1, 4), lax.rem(lon + 3, 4)
+    lat_up, lat_down = lax.rem(lat + 1, 4), lax.rem(lat + 3, 4)
+
+    barrier = pltpu.get_barrier_semaphore()
+    partners = [(lon, bands[1]), (lon, bands[2]), (lon, bands[3]), (across, lat)]
+    for side in (lon_up, lon_down):
+        for band in (lat_down, lat, lat_up):
+            partners.append((side, band))
+
+    def edge_copy(t):
+        rows = pl.ds(pl.multiple_of(t * TILE, TILE), TILE)
+        return pltpu.make_async_copy(edges_ref.at[rows], edge_buf.at[rows], edge_sem.at[t])
+
+    def message_copy(t):
+        rows = pl.ds(pl.multiple_of(t * TILE, TILE), TILE)
+        return pltpu.make_async_copy(message_buf.at[rows], message_ref.at[rows], message_sem.at[t])
+
+    halo_base = nodes
+    lat_base = nodes + 6 * RIM_LON
+    recv_base = nodes + HALO
+    table[pl.ds(nodes, HALO), :] = jnp.zeros((HALO, width), jnp.bfloat16)
+    for other_lon, other_lat in partners:
+        pl.semaphore_signal(
+            barrier, inc=1, device_id={"lon": other_lon, "lat": other_lat}, device_id_type=MESH
+        )
+    for t in range(tiles):
+        edge_copy(t).start()
+
+    senders = (matmul(node_ref[...], edge_in_ref[pl.ds(width, width), :]) * 0.5).astype(jnp.bfloat16)
+    table[pl.ds(0, nodes), :] = senders
+    row_at = lax.broadcasted_iota(jnp.int32, (2 * RIM_LAT, nodes), 0)
+    col_at = lax.broadcasted_iota(jnp.int32, (2 * RIM_LAT, nodes), 1)
+    wanted = jnp.where(
+        row_at < RIM_LAT, row_at * GRID_LAT, (row_at - RIM_LAT) * GRID_LAT + GRID_LAT - 1
+    )
+    picker = jnp.where(col_at == wanted, 1.0, 0.0).astype(jnp.bfloat16)
+    rims[...] = matmul(picker, senders).astype(jnp.bfloat16)
+
+    def remote(src, dst, send, recv, to_lon, to_lat):
+        return pltpu.make_async_remote_copy(
+            src_ref=src,
+            dst_ref=dst,
+            send_sem=send,
+            recv_sem=recv,
+            device_id={"lon": to_lon, "lat": to_lat},
+            device_id_type=MESH,
+        )
+
+    halos = []
+    for side, (to_lon, first) in enumerate(((lon_up, nodes - RIM_LON), (lon_down, 0))):
+        for step, to_lat in enumerate((lat_up, lat, lat_down)):
+            slot = side * 3 + step
+            halos.append(
+                remote(
+                    table.at[pl.ds(first, RIM_LON)],
+                    table.at[pl.ds(halo_base + slot * RIM_LON, RIM_LON)],
+                    halo_send.at[slot],
+                    halo_recv.at[slot],
+                    to_lon,
+                    to_lat,
+                )
+            )
+    for side, (to_lat, first) in enumerate(((lat_up, RIM_LAT), (lat_down, 0))):
+        slot = 6 + side
+        halos.append(
+            remote(
+                rims.at[pl.ds(first, RIM_LAT)],
+                table.at[pl.ds(lat_base + side * RIM_LAT, RIM_LAT)],
+                halo_send.at[slot],
+                halo_recv.at[slot],
+                lon,
+                to_lat,
+            )
+        )
+
+    def block(owner_lon, owner_lat):
+        at = (owner_lon * 4 + owner_lat) * GROUP
+        return every_ref.at[pl.ds(pl.multiple_of(at, GROUP), GROUP)]
+
+    def share(number, owner_lon, owner_lat, to_lon, to_lat):
+        dst = block(owner_lon, owner_lat)
+        src = table.at[pl.ds(0, GROUP)] if number < 5 else dst
+        return remote(
+            src, dst, send_sem.at[number], recv_sem.at[owner_lon * 4 + owner_lat], to_lon, to_lat
+        )
+
+    def arrived(owner_lon, owner_lat):
+        share(5, owner_lon, owner_lat, twin, lat).wait_recv()
+
+    own = [
+        share(0, lon, lat, across, lat),
+        share(1, lon, lat, lon, bands[1]),
+        share(2, lon, lat, lon, bands[2]),
+        share(3, lon, lat, lon, bands[3]),
+        share(4, lon, lat, twin, lat),
+    ]
+    to_across = [None] + [share(4 + k, lon, bands[k], across, lat) for k in (1, 2, 3)]
+    to_twin = [None] + [share(7 + k, lon, bands[k], twin, lat) for k in (1, 2, 3)]
+    passed = [share(11 + k, across, bands[k], twin, lat) for k in (0, 1, 2, 3)]
+
+    def from_band(k):
+        arrived(lon, bands[k])
+        to_across[k].start()
+        to_twin[k].start()
+
+    def from_across(k):
+        arrived(across, bands[k])
+        passed[k].start()
+
+    pl.semaphore_wait(barrier, len(partners))
+    for copy in halos:
+        copy.start()
+    for copy in own:
+        copy.start()
+    keep = pltpu.make_async_copy(table.at[pl.ds(0, GROUP)], block(lon, lat), own_sem)
+    keep.start()
+
+    receivers = (matmul(node_ref[...], edge_in_ref[pl.ds(2 * width, width), :]) * 0.5).astype(
+        jnp.bfloat16
+    )
+    table[pl.ds(recv_base, nodes), :] = receivers
+    recv_table_ref[...] = receivers
+    edge_half[...] = edge_in_ref[pl.ds(0, width), :] * jnp.bfloat16(0.5)
+    total_ref[...] = jnp.zeros_like(total_ref)
+
+    source = lax.shift_right_logical(sender_ref[...], 9)
+    row = lax.bitwise_and(sender_ref[...], 511)
+    lon_shift = lax.bitwise_and(lax.shift_right_logical(source, 2) - lon + 4, 3)
+    lat_shift = lax.bitwise_and(source, 3) - lat
+    near_lon = (
+        halo_base
+        + (jnp.where(lon_shift == 3, 0, 3) + lat_shift + 1) * RIM_LON
+        + lax.bitwise_and(row, GRID_LAT - 1)
+    )
+    near_lat = (
+        lat_base
+        + jnp.where(lat_shift == -1, 0, RIM_LAT)
+        + lax.shift_right_logical(row, 4)
+    )
+    local = jnp.where(lon_shift != 0, near_lon, jnp.where(lat_shift != 0, near_lat, row))
+    sender_ids[...] = local.astype(jnp.float32)
+    receiver_ids[...] = receiver_ref[...].astype(jnp.float32)
+
+    for copy in halos:
+        copy.wait_recv()
+
+    groups = TILE // GROUP
+    per_sub = SUB // GROUP
+
+    def tile(t, carry):
+        @pl.when(t == 1)
+        def _():
+            from_band(1)
+
+        @pl.when(t == 2)
+        def _():
+            from_band(2)
+            from_across(0)
+
+        @pl.when(t == 3)
+        def _():
+            from_band(3)
+            from_across(1)
+
+        @pl.when(t == 5)
+        def _():
+            from_across(2)
+
+        edge_copy(t).wait()
+        to_rows = []
+        for part in range(TILE // SUB):
+            first = t * TILE + part * SUB
+            rows = pl.ds(pl.multiple_of(first, SUB), SUB)
+            ids = [sender_ids[pl.ds(t * groups + part * per_sub + g, 1), :] for g in range(per_sub)]
+            tos = [
+                receiver_ids[pl.ds(t * groups + part * per_sub + g, 1), :] for g in range(per_sub)
+            ]
+            to_rows += tos
+            picks = jnp.concatenate([one_hot(ids, nodes + HALO), one_hot(tos, nodes)], axis=1)
+            half = matmul(edge_buf[rows, :], edge_half[...]) + matmul(picks, table[...])
+            change = normed(matmul(silu_of_twice(half), edge_out_ref[...]), gain_ref[...])
+            message_buf[rows, :] = change.astype(jnp.bfloat16)
+        message_copy(t).start()
+        spread = one_hot_across(to_rows, nodes)
+        rows = pl.ds(pl.multiple_of(t * TILE, TILE), TILE)
+        total_ref[...] += matmul(spread, message_buf[rows, :])
+        return carry
+
+    lax.fori_loop(0, tiles, tile, 0)
+    from_across(3)
+    for band in bands:
+        arrived(twin, band)
+        arrived(lax.rem(twin + 2, 4), band)
+    for copy in halos + own + to_across[1:] + to_twin[1:] + passed:
+        copy.wait_send()
+    keep.wait()
+    for t in range(tiles):
+        message_copy(t).wait()
+
+
+def last_kernel(
+    fine_ref,
+    message_ref,
+    coarse_ref,
+    sender_ref,
+    receiver_ref,
+    every_ref,
+    recv_table_ref,
+    total_ref,
+    edge_in_ref,
+    edge_out_ref,
+    gain_ref,
+    node_ref,
+    node_in_ref,
+    node_out_ref,
+    node_gain_ref,
+    fine_next_ref,
+    coarse_next_ref,
+    node_next_ref,
+    total,
+):
+    step = pl.program_id(0)
+    nodes, width = node_ref.shape
+
+    @pl.when(step == 0)
+    def _():
+        total[...] = total_ref[...]
+
+    fine_next_ref[...] = (
+        fine_ref[...].astype(jnp.float32) + message_ref[...].astype(jnp.float32)
+    ).astype(jnp.bfloat16)
+    per = coarse_ref.shape[0] // GROUP
+    ids = [sender_ref[pl.ds(step * per + g, 1), :].astype(jnp.float32) for g in range(per)]
+    tos = [receiver_ref[pl.ds(step * per + g, 1), :].astype(jnp.float32) for g in range(per)]
+    edges = coarse_ref[...]
+    half = (
+        matmul(edges, edge_in_ref[...]) * 0.5
+        + matmul(one_hot(ids, every_ref.shape[0]), every_ref[...])
+        + matmul(one_hot(tos, nodes), recv_table_ref[...])
+    )
+    change = normed(matmul(silu_of_twice(half), edge_out_ref[...]), gain_ref[...])
+    coarse_next_ref[...] = (edges.astype(jnp.float32) + change).astype(jnp.bfloat16)
+    total[...] += matmul(one_hot_across(tos, nodes), change.astype(jnp.bfloat16))
+
+    @pl.when(step == pl.num_programs(0) - 1)
+    def _():
+        own = node_ref[...]
+        inner = matmul(own, node_in_ref[pl.ds(0, width), :]) + matmul(
+            total[...].astype(jnp.bfloat16), node_in_ref[pl.ds(width, width), :]
+        )
+        moved = normed(matmul(silu_of_twice(inner * 0.5), node_out_ref[...]), node_gain_ref[...])
+        node_next_ref[...] = (own.astype(jnp.float32) + moved).astype(jnp.bfloat16)
+
+
+def fast_shards(
+    node_latent,
+    fine_edges,
+    coarse_edges,
+    fine_sender,
+    fine_receiver,
+    coarse_peer,
+    coarse_row,
+    coarse_receiver,
+    edge_in,
+    edge_out,
+    edge_gain,
+    node_in,
+    node_out,
+    node_gain,
+):
+    nodes, width = node_latent.shape
+    fine = fine_edges.shape[0]
+    coarse = coarse_edges.shape[0]
+    everyone = 16 * GROUP
+    tiles = fine // TILE
+    vmem = pl.BlockSpec(memory_space=pltpu.VMEM)
+    hbm = pl.BlockSpec(memory_space=pl.ANY)
+    table_rows = 2 * nodes + HALO
+    dma = pltpu.SemaphoreType.DMA
+    message, total, every, recv_table = pl.pallas_call(
+        fine_kernel,
+        out_shape=(
+            jax.ShapeDtypeStruct((fine, width), jnp.bfloat16),
+            jax.ShapeDtypeStruct((nodes, width), jnp.float32),
+            jax.ShapeDtypeStruct((everyone, width), jnp.bfloat16),
+            jax.ShapeDtypeStruct((nodes, width), jnp.bfloat16),
+        ),
+        in_specs=[vmem, hbm, vmem, vmem, vmem, vmem, vmem],
+        out_specs=(hbm, vmem, hbm, vmem),
+        scratch_shapes=[
+            pltpu.VMEM((table_rows, width), jnp.bfloat16),
+            pltpu.VMEM((2 * RIM_LAT, width), jnp.bfloat16),
+            pltpu.VMEM((width, width), jnp.bfloat16),
+            pltpu.VMEM((fine, width), jnp.bfloat16),
+            pltpu.VMEM((fine, width), jnp.bfloat16),
+            pltpu.VMEM((fine // GROUP, GROUP), jnp.float32),
+            pltpu.VMEM((fine // GROUP, GROUP), jnp.float32),
+            dma((tiles,)),
+            dma((tiles,)),
+            dma,
+            dma((8,)),
+            dma((8,)),
+            dma((15,)),
+            dma((16,)),
+        ],
+        compiler_params=pltpu.CompilerParams(
+            collective_id=0, has_side_effects=True, vmem_limit_bytes=40 * 2**20
+        ),
+        cost_estimate=pl.CostEstimate(
+            flops=10 * 10**9, bytes_accessed=12 * 2**20, transcendentals=fine * width
+        ),
+    )(
+        node_latent,
+        fine_edges,
+        fine_sender.reshape(fine // GROUP, GROUP),
+        fine_receiver.reshape(fine // GROUP, GROUP),
+        edge_in,
+        edge_out,
+        edge_gain.reshape(1, width),
+    )
+    far = coarse_peer.reshape(coarse // GROUP, GROUP) * GROUP + coarse_row.reshape(
+        coarse // GROUP, GROUP
+    )
+    steps = 4
+
+    def rows_of(count):
+        return pl.BlockSpec((count // steps, width), lambda i: (i, 0))
+
+    def whole(shape):
+        return pl.BlockSpec(shape, lambda i: (0, 0))
+
+    fine_next, coarse_next, node_next = pl.pallas_call(
+        last_kernel,
+        grid=(steps,),
+        out_shape=(
+            jax.ShapeDtypeStruct((fine, width), jnp.bfloat16),
+            jax.ShapeDtypeStruct((coarse, width), jnp.bfloat16),
+            jax.ShapeDtypeStruct((nodes, width), jnp.bfloat16),
+        ),
+        in_specs=[
+            rows_of(fine),
+            rows_of(fine),
+            rows_of(coarse),
+            whole((coarse // GROUP, GROUP)),
+            whole((coarse // GROUP, GROUP)),
+            whole((everyone, width)),
+            whole((nodes, width)),
+            whole((nodes, width)),
+            whole((width, width)),
+            whole((width, width)),
+            whole((1, width)),
+            whole((nodes, width)),
+            whole((2 * width, width)),
+            whole((width, width)),
+            whole((1, width)),
+        ],
+        out_specs=(rows_of(fine), rows_of(coarse), whole((nodes, width))),
+        scratch_shapes=[pltpu.VMEM((nodes, width), jnp.float32)],
+        compiler_params=pltpu.CompilerParams(vmem_limit_bytes=40 * 2**20),
+        cost_estimate=pl.CostEstimate(
+            flops=5 * 10**9, bytes_accessed=16 * 2**20, transcendentals=coarse * width
+        ),
+    )(
+        fine_edges,
+        message,
+        coarse_edges,
+        far,
+        coarse_receiver.reshape(coarse // GROUP, GROUP),
+        every,
+        recv_table,
+        total,
+        edge_in,
+        edge_out,
+        edge_gain.reshape(1, width),
+        node_latent,
+        node_in,
+        node_out,
+        node_gain.reshape(1, width),
+    )
+    return (node_next, fine_next, coarse_next)
 
 
 def with_halo(cells, sides, width, closed):
@@ -106,8 +577,9 @@
 
 
 def solution(mesh):
+    small = mesh.shape["lon"] == 4 and mesh.shape["lat"] == 4
     return jax.shard_map(
-        shards,
+        fast_shards if small else shards,
         mesh=mesh,
         in_specs=(
             P(("groups", "lon", "lat"), None),

time: 121 us -> 52.2 us (0.43)
  Pallas kernels: 0 us -> 40.4 us
  matrix products: 38 us -> 0 us
  local copies, waits for them, and re-layouts: 33.5 us -> 9.15 us
  other arithmetic: 14.9 us -> 1.38 us
  between operations: 14.2 us -> 0.73 us
  waiting for transfers between devices: 11.6 us -> 0 us
  starting transfers between devices: 8.19 us -> 0 us
    pallas_call x0 -> x2, Pallas kernels: none -> 40.4 us  [the longest x1 28.4 us: fast_shards(): pl.pallas_call(fine_kernel, out_shape=(jax.ShapeDtypeStruct((fine, width)...]
    dot_general x5 -> x0, matrix products: 38 us -> none  [the longest x1 20.3 us: shards(): jnp.dot(edge_hidden, edge_out, preferred_element_type=jnp.float32)]
    all_gather x1 -> x0, waiting for transfers between devices: 11.6 us -> none  [shards(): lax.all_gather(node_latent[:coarse_count], ('lon', 'lat'), axis=0, tiled=...]
    gather x2 -> x0, local copies, waits for them, and re-layouts: 9.24 us -> none  [shards(): far = jnp.take(everyone, peers * coarse_count + coarse_row, axis=0)]
    ppermute x4 -> x0, starting transfers between devices: 8.15 us -> none  [the longest x2 4.75 us: with_halo(): lax.ppermute(tail, axis, [(i, (i + 1) % count) for i in range(ends)])]
    unnamed x21 -> x32, local copies, waits for them, and re-layouts: 16.9 us -> 9.15 us
    convert_element_type x2 -> x0, other arithmetic: 5 us -> none  [the longest x1 3.74 us: shards(): edge_next = (edges.astype(jnp.float32) + edge_change).astype(jnp.bfloat16)]
    reduce_sum x2 -> x0, other arithmetic: 4.69 us -> none  [layer_norm(): jnp.mean(centred * centred, axis=-1, keepdims=True) + 1e-05]
  transfers between devices with their start and end apart: 5 -> 0, of which waited for: 1 -> 0; matrix products, arithmetic and copies ran while one was open for 21% -> 0% of each run, Pallas kernels for 0% -> 0%
where the time goes in v1:
time: 52.2 us; the launch traced here: 51.7 us
  Pallas kernels  40.4 us (77%)
  local copies, waits for them, and re-layouts  9.15 us (18%)
  other arithmetic  1.38 us (3%)
  between operations  0.73 us (1%)
    pallas_call x1, Pallas kernels, fast_shards(): pl.pallas_call(fine_kernel, out_shape=(jax.ShapeDtypeStruct((fine, width)...  28.4 us
    pallas_call x1, Pallas kernels, fast_shards(): pl.pallas_call(last_kernel, grid=(steps,), out_shape=(jax.ShapeDtypeStruc...  12.1 us
    unnamed x32, local copies, waits for them, and re-layouts  9.15 us

profile of v1, /device:TPU:0, one launch (start us, length us, event | category | flops | bytes accessed | tf_op | source)
XLA Modules:
  0.0 51.7 jit_solution(11879159226545559100)
XLA Ops:
  0.6 0.7 %broadcast_multiply_fusion = s32[1024,1]{0,1:T(1,128)S(1)} fusion(s32[1024,1]{0,1:T(1,128)} %param.19), kind=kLoop, calls=%fused_computation.1 | loop fusion | flops 1024 | bytes 8192 | tf_op jit(solution)/shard_map/mul | solution.py:418
  1.3 0.7 %bitcast_add_fusion.sender_ref = s32[8,128]{1,0:T(8,128)S(1)} fusion(s32[8,128]{1,0:T(8,128)S(1)} %bitcast.14, s32[1024]{0:T(1024)} %param.20), kind=kLoop, calls=%fused_computation | loop fusion | flops 1024 | bytes 12288 | tf_op jit(solution)/shard_map/add | solution.py:418
  2.0 0.0 copy-start
  2.0 1.9 %copy-done = bf16[3072,512]{1,0:T(8,128)(2,1)S(1)} copy-done((bf16[3072,512]{1,0:T(8,128)(2,1)S(1)}, bf16[3072,512]{1,0:T(8,128)(2,1)}, u32[]{:S(2)}) %copy-start) | copy-done | bytes 3145752
  3.9 0.0 copy-start.1
  3.9 1.4 %copy-done.1 = bf16[1536,512]{1,0:T(8,128)(2,1)S(1)} copy-done((bf16[1536,512]{1,0:T(8,128)(2,1)S(1)}, bf16[1536,512]{1,0:T(8,128)(2,1)}, u32[]{:S(2)}) %copy-start.1) | copy-done | bytes 1572888
  5.3 0.0 copy-start.5
  5.3 1.0 %copy-done.5 = bf16[512,512]{1,0:T(8,128)(2,1)S(1)} copy-done((bf16[512,512]{1,0:T(8,128)(2,1)S(1)}, bf16[512,512]{1,0:T(8,128)(2,1)}, u32[]{:S(2)}) %copy-start.5) | copy-done | bytes 524312
  6.4 0.0 copy-start.6
  6.4 1.0 %copy-done.6 = bf16[512,512]{1,0:T(8,128)(2,1)S(1)} copy-done((bf16[512,512]{1,0:T(8,128)(2,1)S(1)}, bf16[512,512]{1,0:T(8,128)(2,1)}, u32[]{:S(2)}) %copy-start.6) | copy-done | bytes 524312
  7.4 0.0 copy-start.9
  7.4 0.7 %copy-done.9 = s32[3072]{0:T(1024)S(1)} copy-done((s32[3072]{0:T(1024)S(1)}, s32[3072]{0:T(1024)}, u32[]{:S(2)}) %copy-start.9) | copy-done | bytes 12312
  8.1 0.0 copy-start.10
  8.1 0.7 %copy-done.10 = s32[3072]{0:T(1024)S(1)} copy-done((s32[3072]{0:T(1024)S(1)}, s32[3072]{0:T(1024)}, u32[]{:S(2)}) %copy-start.10) | copy-done | bytes 12312
  8.8 0.0 copy-start.12
  8.8 0.7 %copy-done.12 = f32[512]{0:T(512)S(1)} copy-done((f32[512]{0:T(512)S(1)}, f32[512]{0:T(512)}, u32[]{:S(2)}) %copy-start.12) | copy-done | bytes 2072
  9.5 0.0 copy-start.2
  9.5 0.0 copy-start.3
  9.5 0.0 copy-start.4
  9.5 0.0 copy-start.7
  9.5 0.0 copy-start.8
  9.5 0.0 copy-start.11
  9.5 0.0 copy-start.13
  9.5 0.0 copy-start.14
  9.5 28.4 %shard_map.157 = (bf16[3072,512]{1,0:T(8,128)(2,1)S(1)}, f32[512,512]{1,0:T(8,128)S(1)}, bf16[2048,512]{1,0:T(8,128)(2,1)S(1)}, bf16[512,512]{1,0:T(8,128)(2,1)S(1)}) custom-call(bf16[512,512]{1,0:T(8,128)(2,1)S(1)} %copy-done.5, bf16[3072,512]{1,0:T(8,128)(2,1)S(1)} %copy-done, s32[24,128]{1,0:T(8,128)S(1)} %bitcast.8, s32[24,128]{1,0:T(8,128)S(1)} %bitcast.9, ...), custom_call_target="tpu_custom_call" | custom-call | flops 10000000000 | bytes 12582912 | tf_op jit(solution)/shard_map/pallas_call | solution.py:377
  37.9 0.0 copy-start.15
  37.9 1.6 %copy-done.15 = bf16[3072,512]{1,0:T(8,128)(2,1)} copy-done((bf16[3072,512]{1,0:T(8,128)(2,1)}, bf16[3072,512]{1,0:T(8,128)(2,1)S(1)}, u32[]{:S(2)}) %copy-start.15) | copy-done | bytes 3145752
  39.6 0.0 copy-done.2
  39.6 0.0 copy-done.3
  39.6 0.0 copy-done.4
  39.6 0.0 copy-done.7
  39.6 0.0 copy-done.8
  39.6 0.0 copy-done.11
  39.6 0.0 copy-done.13
  39.6 0.0 copy-done.14
  39.6 12.1 %shard_map.158 = (bf16[3072,512]{1,0:T(8,128)(2,1)}, bf16[1024,512]{1,0:T(8,128)(2,1)}, bf16[512,512]{1,0:T(8,128)(2,1)}) custom-call(bf16[3072,512]{1,0:T(8,128)(2,1)S(1)} %copy-done, bf16[3072,512]{1,0:T(8,128)(2,1)} %copy-done.15, bf16[1024,512]{1,0:T(8,128)(2,1)S(1)} %copy-done.3, s32[8,128]{1,0:T(8,128)S(1)} %bitcast_add_fusion.sender_ref, ...), custom_call_target="tpu_custom_call" | custom-call | flops 5000000000 | bytes 16777216 | tf_op jit(solution)/shard_map/pallas_call | solution.py:429
Async XLA Ops:
  2.0 1.9 %copy-start = (bf16[3072,512]{1,0:T(8,128)(2,1)S(1)}, bf16[3072,512]{1,0:T(8,128)(2,1)}, u32[]{:S(2)}) copy-start(bf16[3072,512]{1,0:T(8,128)(2,1)} %fine_ref.1) | copy-start | bytes 9437188
  3.9 1.4 %copy-start.1 = (bf16[1536,512]{1,0:T(8,128)(2,1)S(1)}, bf16[1536,512]{1,0:T(8,128)(2,1)}, u32[]{:S(2)}) copy-start(bf16[1536,512]{1,0:T(8,128)(2,1)} %edge_in_ref.3) | copy-start | bytes 4718596
  5.3 1.0 %copy-start.5 = (bf16[512,512]{1,0:T(8,128)(2,1)S(1)}, bf16[512,512]{1,0:T(8,128)(2,1)}, u32[]{:S(2)}) copy-start(bf16[512,512]{1,0:T(8,128)(2,1)} %node_ref.3) | copy-start | bytes 1572868
  6.4 1.0 %copy-start.6 = (bf16[512,512]{1,0:T(8,128)(2,1)S(1)}, bf16[512,512]{1,0:T(8,128)(2,1)}, u32[]{:S(2)}) copy-start(bf16[512,512]{1,0:T(8,128)(2,1)} %edge_out_ref.3) | copy-start | bytes 1572868
  7.4 0.7 %copy-start.9 = (s32[3072]{0:T(1024)S(1)}, s32[3072]{0:T(1024)}, u32[]{:S(2)}) copy-start(s32[3072]{0:T(1024)} %param.17) | copy-start | bytes 36868
  8.1 0.7 %copy-start.10 = (s32[3072]{0:T(1024)S(1)}, s32[3072]{0:T(1024)}, u32[]{:S(2)}) copy-start(s32[3072]{0:T(1024)} %param.18) | copy-start | bytes 36868
  8.8 0.7 %copy-start.12 = (f32[512]{0:T(512)S(1)}, f32[512]{0:T(512)}, u32[]{:S(2)}) copy-start(f32[512]{0:T(512)} %param.24) | copy-start | bytes 6148
  9.5 30.1 %copy-start.2 = (bf16[1536,512]{1,0:T(8,128)(2,1)S(1)}, bf16[1536,512]{1,0:T(8,128)(2,1)}, u32[]{:S(2)}) copy-start(bf16[1536,512]{1,0:T(8,128)(2,1)} %edge_in_ref.3) | copy-start | bytes 4718596
  9.5 30.1 %copy-start.3 = (bf16[1024,512]{1,0:T(8,128)(2,1)S(1)}, bf16[1024,512]{1,0:T(8,128)(2,1)}, u32[]{:S(2)}) copy-start(bf16[1024,512]{1,0:T(8,128)(2,1)} %coarse_ref.1) | copy-start | bytes 3145732
  9.5 30.1 %copy-start.4 = (bf16[1024,512]{1,0:T(8,128)(2,1)S(1)}, bf16[1024,512]{1,0:T(8,128)(2,1)}, u32[]{:S(2)}) copy-start(bf16[1024,512]{1,0:T(8,128)(2,1)} %node_in_ref.1) | copy-start | bytes 3145732
  9.5 30.1 %copy-start.7 = (bf16[512,512]{1,0:T(8,128)(2,1)S(1)}, bf16[512,512]{1,0:T(8,128)(2,1)}, u32[]{:S(2)}) copy-start(bf16[512,512]{1,0:T(8,128)(2,1)} %edge_out_ref.3) | copy-start | bytes 1572868
  9.5 30.1 %copy-start.8 = (bf16[512,512]{1,0:T(8,128)(2,1)S(1)}, bf16[512,512]{1,0:T(8,128)(2,1)}, u32[]{:S(2)}) copy-start(bf16[512,512]{1,0:T(8,128)(2,1)} %node_out_ref.1) | copy-start | bytes 1572868
  9.5 30.1 %copy-start.11 = (s32[1024]{0:T(1024)S(1)}, s32[1024]{0:T(1024)}, u32[]{:S(2)}) copy-start(s32[1024]{0:T(1024)} %param.21) | copy-start | bytes 12292
  9.5 30.1 %copy-start.13 = (f32[512]{0:T(512)S(1)}, f32[512]{0:T(512)}, u32[]{:S(2)}) copy-start(f32[512]{0:T(512)} %param.24) | copy-start | bytes 6148
  9.5 30.1 %copy-start.14 = (f32[512]{0:T(512)S(1)}, f32[512]{0:T(512)}, u32[]{:S(2)}) copy-start(f32[512]{0:T(512)} %param.27) | copy-start | bytes 6148
  37.9 1.7 %copy-start.15 = (bf16[3072,512]{1,0:T(8,128)(2,1)}, bf16[3072,512]{1,0:T(8,128)(2,1)S(1)}, u32[]{:S(2)}) copy-start(bf16[3072,512]{1,0:T(8,128)(2,1)S(1)} %get-tuple-element.10.message_ref) | copy-start | bytes 9437188

commit v2 on v1

--- a/solution.py
+++ b/solution.py
@@ -9,7 +9,8 @@
 MESH = pl.DeviceIdType.MESH
 GROUP = 128
 TILE = 512
-SUB = 256
+SUB = 512
+LAST = 512
 RIM_LON = 16
 RIM_LAT = 32
 HALO = 256
@@ -63,19 +64,24 @@
     edge_in_ref,
     edge_out_ref,
     gain_ref,
-    message_ref,
+    fine_next_ref,
     total_ref,
     every_ref,
     recv_table_ref,
+    node,
+    thirds,
+    edge_out,
+    gain,
+    sender,
+    receiver,
     table,
     rims,
     edge_half,
     edge_buf,
-    message_buf,
     sender_ids,
     receiver_ids,
     edge_sem,
-    message_sem,
+    load_sem,
     own_sem,
     halo_send,
     halo_recv,
@@ -108,9 +114,27 @@
         rows = pl.ds(pl.multiple_of(t * TILE, TILE), TILE)
         return pltpu.make_async_copy(edges_ref.at[rows], edge_buf.at[rows], edge_sem.at[t])
 
-    def message_copy(t):
-        rows = pl.ds(pl.multiple_of(t * TILE, TILE), TILE)
-        return pltpu.make_async_copy(message_buf.at[rows], message_ref.at[rows], message_sem.at[t])
+    def third(k):
+        rows = pl.ds(k * width, width)
+        return edge_in_ref.at[rows], thirds.at[rows]
+
+    loads = [
+        pltpu.make_async_copy(src, dst, load_sem.at[k])
+        for k, (src, dst) in enumerate(
+            (
+                (node_ref, node),
+                third(1),
+                third(2),
+                third(0),
+                (sender_ref, sender),
+                (receiver_ref, receiver),
+                (edge_out_ref, edge_out),
+                (gain_ref, gain),
+            )
+        )
+    ]
+    for load in loads[:2]:
+        load.start()
 
     halo_base = nodes
     lat_base = nodes + 6 * RIM_LON
@@ -120,10 +144,14 @@
         pl.semaphore_signal(
             barrier, inc=1, device_id={"lon": other_lon, "lat": other_lat}, device_id_type=MESH
         )
+    for load in loads[2:]:
+        load.start()
     for t in range(tiles):
         edge_copy(t).start()
-
-    senders = (matmul(node_ref[...], edge_in_ref[pl.ds(width, width), :]) * 0.5).astype(jnp.bfloat16)
+    for load in loads[:2]:
+        load.wait()
+
+    senders = (matmul(node[...], thirds[pl.ds(width, width), :]) * 0.5).astype(jnp.bfloat16)
     table[pl.ds(0, nodes), :] = senders
     row_at = lax.broadcasted_iota(jnp.int32, (2 * RIM_LAT, nodes), 0)
     col_at = lax.broadcasted_iota(jnp.int32, (2 * RIM_LAT, nodes), 1)
@@ -212,16 +240,18 @@
     keep = pltpu.make_async_copy(table.at[pl.ds(0, GROUP)], block(lon, lat), own_sem)
     keep.start()
 
-    receivers = (matmul(node_ref[...], edge_in_ref[pl.ds(2 * width, width), :]) * 0.5).astype(
+    for load in loads[2:]:
+        load.wait()
+    receivers = (matmul(node[...], thirds[pl.ds(2 * width, width), :]) * 0.5).astype(
         jnp.bfloat16
     )
     table[pl.ds(recv_base, nodes), :] = receivers
     recv_table_ref[...] = receivers
-    edge_half[...] = edge_in_ref[pl.ds(0, width), :] * jnp.bfloat16(0.5)
+    edge_half[...] = thirds[pl.ds(0, width), :] * jnp.bfloat16(0.5)
     total_ref[...] = jnp.zeros_like(total_ref)
 
-    source = lax.shift_right_logical(sender_ref[...], 9)
-    row = lax.bitwise_and(sender_ref[...], 511)
+    source = lax.shift_right_logical(sender[...], 9)
+    row = lax.bitwise_and(sender[...], 511)
     lon_shift = lax.bitwise_and(lax.shift_right_logical(source, 2) - lon + 4, 3)
     lat_shift = lax.bitwise_and(source, 3) - lat
     near_lon = (
@@ -236,7 +266,7 @@
     )
     local = jnp.where(lon_shift != 0, near_lon, jnp.where(lat_shift != 0, near_lat, row))
     sender_ids[...] = local.astype(jnp.float32)
-    receiver_ids[...] = receiver_ref[...].astype(jnp.float32)
+    receiver_ids[...] = receiver[...].astype(jnp.float32)
 
     for copy in halos:
         copy.wait_recv()
@@ -264,7 +294,7 @@
             from_across(2)
 
         edge_copy(t).wait()
-        to_rows = []
+        to_rows, messages = [], []
         for part in range(TILE // SUB):
             first = t * TILE + part * SUB
             rows = pl.ds(pl.multiple_of(first, SUB), SUB)
@@ -274,13 +304,13 @@
             ]
             to_rows += tos
             picks = jnp.concatenate([one_hot(ids, nodes + HALO), one_hot(tos, nodes)], axis=1)
-            half = matmul(edge_buf[rows, :], edge_half[...]) + matmul(picks, table[...])
-            change = normed(matmul(silu_of_twice(half), edge_out_ref[...]), gain_ref[...])
-            message_buf[rows, :] = change.astype(jnp.bfloat16)
-        message_copy(t).start()
+            edges = edge_buf[rows, :]
+            half = matmul(edges, edge_half[...]) + matmul(picks, table[...])
+            change = normed(matmul(silu_of_twice(half), edge_out[...]), gain[...])
+            fine_next_ref[rows, :] = (edges.astype(jnp.float32) + change).astype(jnp.bfloat16)
+            messages.append(change.astype(jnp.bfloat16))
         spread = one_hot_across(to_rows, nodes)
-        rows = pl.ds(pl.multiple_of(t * TILE, TILE), TILE)
-        total_ref[...] += matmul(spread, message_buf[rows, :])
+        total_ref[...] += matmul(spread, jnp.concatenate(messages, axis=0))
         return carry
 
     lax.fori_loop(0, tiles, tile, 0)
@@ -291,15 +321,13 @@
     for copy in halos + own + to_across[1:] + to_twin[1:] + passed:
         copy.wait_send()
     keep.wait()
-    for t in range(tiles):
-        message_copy(t).wait()
 
 
 def last_kernel(
     fine_ref,
-    message_ref,
     coarse_ref,
-    sender_ref,
+    peer_ref,
+    row_ref,
     receiver_ref,
     every_ref,
     recv_table_ref,
@@ -314,39 +342,44 @@
     fine_next_ref,
     coarse_next_ref,
     node_next_ref,
-    total,
+    coarse_buf,
+    out_sem,
 ):
-    step = pl.program_id(0)
     nodes, width = node_ref.shape
-
-    @pl.when(step == 0)
-    def _():
-        total[...] = total_ref[...]
-
-    fine_next_ref[...] = (
-        fine_ref[...].astype(jnp.float32) + message_ref[...].astype(jnp.float32)
-    ).astype(jnp.bfloat16)
-    per = coarse_ref.shape[0] // GROUP
-    ids = [sender_ref[pl.ds(step * per + g, 1), :].astype(jnp.float32) for g in range(per)]
-    tos = [receiver_ref[pl.ds(step * per + g, 1), :].astype(jnp.float32) for g in range(per)]
-    edges = coarse_ref[...]
-    half = (
-        matmul(edges, edge_in_ref[...]) * 0.5
-        + matmul(one_hot(ids, every_ref.shape[0]), every_ref[...])
-        + matmul(one_hot(tos, nodes), recv_table_ref[...])
-    )
-    change = normed(matmul(silu_of_twice(half), edge_out_ref[...]), gain_ref[...])
-    coarse_next_ref[...] = (edges.astype(jnp.float32) + change).astype(jnp.bfloat16)
-    total[...] += matmul(one_hot_across(tos, nodes), change.astype(jnp.bfloat16))
-
-    @pl.when(step == pl.num_programs(0) - 1)
-    def _():
-        own = node_ref[...]
-        inner = matmul(own, node_in_ref[pl.ds(0, width), :]) + matmul(
-            total[...].astype(jnp.bfloat16), node_in_ref[pl.ds(width, width), :]
-        )
-        moved = normed(matmul(silu_of_twice(inner * 0.5), node_out_ref[...]), node_gain_ref[...])
-        node_next_ref[...] = (own.astype(jnp.float32) + moved).astype(jnp.bfloat16)
+    count = coarse_ref.shape[0]
+    fine_out = pltpu.make_async_copy(fine_ref, fine_next_ref, out_sem.at[0])
+    fine_out.start()
+    far = (peer_ref[...] * GROUP + row_ref[...]).astype(jnp.float32)
+    to = receiver_ref[...].astype(jnp.float32)
+    per = LAST // GROUP
+    outs = [fine_out]
+    total = total_ref[...]
+    for part in range(count // LAST):
+        ids = [far[part * per + g : part * per + g + 1, :] for g in range(per)]
+        tos = [to[part * per + g : part * per + g + 1, :] for g in range(per)]
+        rows = pl.ds(part * LAST, LAST)
+        edges = coarse_ref[rows, :]
+        half = (
+            matmul(edges, edge_in_ref[pl.ds(0, width), :]) * 0.5
+            + matmul(one_hot(ids, every_ref.shape[0]), every_ref[...])
+            + matmul(one_hot(tos, nodes), recv_table_ref[...])
+        )
+        change = normed(matmul(silu_of_twice(half), edge_out_ref[...]), gain_ref[...])
+        coarse_buf[rows, :] = (edges.astype(jnp.float32) + change).astype(jnp.bfloat16)
+        out = pltpu.make_async_copy(
+            coarse_buf.at[rows], coarse_next_ref.at[rows], out_sem.at[part + 1]
+        )
+        out.start()
+        outs.append(out)
+        total = total + matmul(one_hot_across(tos, nodes), change.astype(jnp.bfloat16))
+    own = node_ref[...]
+    inner = matmul(own, node_in_ref[pl.ds(0, width), :]) + matmul(
+        total.astype(jnp.bfloat16), node_in_ref[pl.ds(width, width), :]
+    )
+    moved = normed(matmul(silu_of_twice(inner * 0.5), node_out_ref[...]), node_gain_ref[...])
+    node_next_ref[...] = (own.astype(jnp.float32) + moved).astype(jnp.bfloat16)
+    for out in outs:
+        out.wait()
 
 
 def fast_shards(
@@ -371,10 +404,10 @@
     everyone = 16 * GROUP
     tiles = fine // TILE
     vmem = pl.BlockSpec(memory_space=pltpu.VMEM)
-    hbm = pl.BlockSpec(memory_space=pl.ANY)
+    hbm = pl.BlockSpec(memory_space=pltpu.HBM)
     table_rows = 2 * nodes + HALO
     dma = pltpu.SemaphoreType.DMA
-    message, total, every, recv_table = pl.pallas_call(
+    fine_made, total, every, recv_table = pl.pallas_call(
         fine_kernel,
         out_shape=(
             jax.ShapeDtypeStruct((fine, width), jnp.bfloat16),
@@ -382,18 +415,23 @@
             jax.ShapeDtypeStruct((everyone, width), jnp.bfloat16),
             jax.ShapeDtypeStruct((nodes, width), jnp.bfloat16),
         ),
-        in_specs=[vmem, hbm, vmem, vmem, vmem, vmem, vmem],
-        out_specs=(hbm, vmem, hbm, vmem),
+        in_specs=[hbm] * 7,
+        out_specs=(vmem,) * 4,
         scratch_shapes=[
+            pltpu.VMEM((nodes, width), jnp.bfloat16),
+            pltpu.VMEM((3 * width, width), jnp.bfloat16),
+            pltpu.VMEM((width, width), jnp.bfloat16),
+            pltpu.VMEM((1, width), jnp.float32),
+            pltpu.VMEM((fine // GROUP, GROUP), jnp.int32),
+            pltpu.VMEM((fine // GROUP, GROUP), jnp.int32),
             pltpu.VMEM((table_rows, width), jnp.bfloat16),
             pltpu.VMEM((2 * RIM_LAT, width), jnp.bfloat16),
             pltpu.VMEM((width, width), jnp.bfloat16),
             pltpu.VMEM((fine, width), jnp.bfloat16),
-            pltpu.VMEM((fine, width), jnp.bfloat16),
             pltpu.VMEM((fine // GROUP, GROUP), jnp.float32),
             pltpu.VMEM((fine // GROUP, GROUP), jnp.float32),
             dma((tiles,)),
-            dma((tiles,)),
+            dma((8,)),
             dma,
             dma((8,)),
             dma((8,)),
@@ -401,67 +439,47 @@
             dma((16,)),
         ],
         compiler_params=pltpu.CompilerParams(
-            collective_id=0, has_side_effects=True, vmem_limit_bytes=40 * 2**20
+            collective_id=0, has_side_effects=True, vmem_limit_bytes=36 * 2**20
         ),
         cost_estimate=pl.CostEstimate(
             flops=10 * 10**9, bytes_accessed=12 * 2**20, transcendentals=fine * width
         ),
     )(
-        node_latent,
-        fine_edges,
-        fine_sender.reshape(fine // GROUP, GROUP),
-        fine_receiver.reshape(fine // GROUP, GROUP),
-        edge_in,
-        edge_out,
-        edge_gain.reshape(1, width),
-    )
-    far = coarse_peer.reshape(coarse // GROUP, GROUP) * GROUP + coarse_row.reshape(
-        coarse // GROUP, GROUP
-    )
-    steps = 4
-
-    def rows_of(count):
-        return pl.BlockSpec((count // steps, width), lambda i: (i, 0))
-
-    def whole(shape):
-        return pl.BlockSpec(shape, lambda i: (0, 0))
-
+        *[
+            pltpu.with_memory_space_constraint(operand, pltpu.HBM)
+            for operand in (
+                node_latent,
+                fine_edges,
+                fine_sender.reshape(fine // GROUP, GROUP),
+                fine_receiver.reshape(fine // GROUP, GROUP),
+                edge_in,
+                edge_out,
+                edge_gain.reshape(1, width),
+            )
+        ]
+    )
     fine_next, coarse_next, node_next = pl.pallas_call(
         last_kernel,
-        grid=(steps,),
         out_shape=(
             jax.ShapeDtypeStruct((fine, width), jnp.bfloat16),
             jax.ShapeDtypeStruct((coarse, width), jnp.bfloat16),
             jax.ShapeDtypeStruct((nodes, width), jnp.bfloat16),
         ),
-        in_specs=[
-            rows_of(fine),
-            rows_of(fine),
-            rows_of(coarse),
-            whole((coarse // GROUP, GROUP)),
-            whole((coarse // GROUP, GROUP)),
-            whole((everyone, width)),
-            whole((nodes, width)),
-            whole((nodes, width)),
-            whole((width, width)),
-            whole((width, width)),
-            whole((1, width)),
-            whole((nodes, width)),
-            whole((2 * width, width)),
-            whole((width, width)),
-            whole((1, width)),
+        in_specs=[vmem] * 15,
+        out_specs=(hbm, hbm, vmem),
+        scratch_shapes=[
+            pltpu.VMEM((coarse, width), jnp.bfloat16),
+            dma((1 + coarse // LAST,)),
         ],
-        out_specs=(rows_of(fine), rows_of(coarse), whole((nodes, width))),
-        scratch_shapes=[pltpu.VMEM((nodes, width), jnp.float32)],
-        compiler_params=pltpu.CompilerParams(vmem_limit_bytes=40 * 2**20),
+        compiler_params=pltpu.CompilerParams(vmem_limit_bytes=36 * 2**20),
         cost_estimate=pl.CostEstimate(
             flops=5 * 10**9, bytes_accessed=16 * 2**20, transcendentals=coarse * width
         ),
     )(
-        fine_edges,
-        message,
+        fine_made,
         coarse_edges,
-        far,
+        coarse_peer.reshape(coarse // GROUP, GROUP),
+        coarse_row.reshape(coarse // GROUP, GROUP),
         coarse_receiver.reshape(coarse // GROUP, GROUP),
         every,
         recv_table,

time: 52.2 us -> 36.4 us (0.70)
  local copies, waits for them, and re-layouts: 9.15 us -> 0.05 us
  Pallas kernels: 40.4 us -> 35.4 us
  other arithmetic: 1.38 us -> 0 us
    unnamed x32 -> x22, local copies, waits for them, and re-layouts: 9.15 us -> 0.05 us
    pallas_call x1, Pallas kernels: 12.1 us -> 7.24 us  [fast_shards(): pl.pallas_call(last_kernel, out_shape=(jax.ShapeDtypeStruct((fine, width)...]
    mul x1 -> x0, other arithmetic: 0.69 us -> none  [fast_shards(): coarse_peer.reshape(coarse // GROUP, GROUP) * GROUP]
    add x1 -> x0, other arithmetic: 0.69 us -> none  [fast_shards(): coarse_peer.reshape(coarse // GROUP, GROUP) * GROUP]
where the time goes in v2:
time: 36.4 us; the launch traced here: 36.3 us
  Pallas kernels  35.4 us (97%)
  between operations  0.82 us (2%)
    pallas_call x1, Pallas kernels, fast_shards(): pl.pallas_call(fine_kernel, out_shape=(jax.ShapeDtypeStruct((fine, width)...  28.2 us
    pallas_call x1, Pallas kernels, fast_shards(): pl.pallas_call(last_kernel, out_shape=(jax.ShapeDtypeStruct((fine, width)...  7.24 us

profile of v2, /device:TPU:0, one launch (start us, length us, event | category | flops | bytes accessed | tf_op | source)
XLA Modules:
  0.0 36.3 jit_solution(15019550129699521870)
XLA Ops:
  0.6 0.0 copy-start
  0.6 0.0 copy-start.1
  0.7 0.0 copy-start.2
  0.7 0.0 copy-start.3
  0.7 0.0 copy-start.4
  0.7 0.0 copy-start.5
  0.7 0.0 copy-start.6
  0.7 0.0 copy-start.7
  0.7 0.0 copy-start.8
  0.7 0.0 copy-start.9
  0.7 0.0 copy-start.10
  0.7 28.2 %shard_map.157 = (bf16[3072,512]{1,0:T(8,128)(2,1)S(1)}, f32[512,512]{1,0:T(8,128)S(1)}, bf16[2048,512]{1,0:T(8,128)(2,1)S(1)}, bf16[512,512]{1,0:T(8,128)(2,1)S(1)}) custom-call(bf16[512,512]{1,0:T(8,128)(2,1)} %node_ref.3, bf16[3072,512]{1,0:T(8,128)(2,1)} %edges_ref.1, s32[24,128]{1,0:T(8,128)} %bitcast.13, s32[24,128]{1,0:T(8,128)} %bitcast.14, ...), custom_call_target="tpu_custom_call" | custom-call | flops 10000000000 | bytes 12582912 | tf_op jit(solution)/shard_map/pallas_call | solution.py:410
  28.9 0.0 copy-done
  28.9 0.0 copy-done.1
  28.9 0.0 copy-done.2
  28.9 0.0 copy-done.3
  28.9 0.0 copy-done.4
  29.0 0.0 copy-done.5
  29.0 0.0 copy-done.6
  29.0 0.0 copy-done.7
  29.0 0.0 copy-done.8
  29.0 0.0 copy-done.9
  29.0 0.0 copy-done.10
  29.0 7.2 %shard_map.158 = (bf16[3072,512]{1,0:T(8,128)(2,1)}, bf16[1024,512]{1,0:T(8,128)(2,1)}, bf16[512,512]{1,0:T(8,128)(2,1)}) custom-call(bf16[3072,512]{1,0:T(8,128)(2,1)S(1)} %get-tuple-element.10.fine_ref, bf16[1024,512]{1,0:T(8,128)(2,1)S(1)} %copy-done.1, s32[8,128]{1,0:T(8,128)S(1)} %bitcast.7, s32[8,128]{1,0:T(8,128)S(1)} %bitcast.8, ...), custom_call_target="tpu_custom_call" | custom-call | flops 5000000000 | bytes 16777216 | tf_op jit(solution)/shard_map/pallas_call | solution.py:461
Async XLA Ops:
  0.6 28.3 %copy-start = (bf16[1536,512]{1,0:T(8,128)(2,1)S(1)}, bf16[1536,512]{1,0:T(8,128)(2,1)}, u32[]{:S(2)}) copy-start(bf16[1536,512]{1,0:T(8,128)(2,1)} %edge_in_ref.3) | copy-start | bytes 4718596
  0.6 28.3 %copy-start.1 = (bf16[1024,512]{1,0:T(8,128)(2,1)S(1)}, bf16[1024,512]{1,0:T(8,128)(2,1)}, u32[]{:S(2)}) copy-start(bf16[1024,512]{1,0:T(8,128)(2,1)} %coarse_ref.1) | copy-start | bytes 3145732
  0.7 28.3 %copy-start.2 = (bf16[1024,512]{1,0:T(8,128)(2,1)S(1)}, bf16[1024,512]{1,0:T(8,128)(2,1)}, u32[]{:S(2)}) copy-start(bf16[1024,512]{1,0:T(8,128)(2,1)} %node_in_ref.1) | copy-start | bytes 3145732
  0.7 28.3 %copy-start.3 = (bf16[512,512]{1,0:T(8,128)(2,1)S(1)}, bf16[512,512]{1,0:T(8,128)(2,1)}, u32[]{:S(2)}) copy-start(bf16[512,512]{1,0:T(8,128)(2,1)} %node_ref.3) | copy-start | bytes 1572868
  0.7 28.3 %copy-start.4 = (bf16[512,512]{1,0:T(8,128)(2,1)S(1)}, bf16[512,512]{1,0:T(8,128)(2,1)}, u32[]{:S(2)}) copy-start(bf16[512,512]{1,0:T(8,128)(2,1)} %edge_out_ref.3) | copy-start | bytes 1572868
  0.7 28.3 %copy-start.5 = (bf16[512,512]{1,0:T(8,128)(2,1)S(1)}, bf16[512,512]{1,0:T(8,128)(2,1)}, u32[]{:S(2)}) copy-start(bf16[512,512]{1,0:T(8,128)(2,1)} %node_out_ref.1) | copy-start | bytes 1572868
  0.7 28.3 %copy-start.6 = (s32[1024,1]{0,1:T(1,128)S(1)}, s32[1024,1]{0,1:T(1,128)}, u32[]{:S(2)}) copy-start(s32[1024,1]{0,1:T(1,128)} %param.19) | copy-start | bytes 12292
  0.7 28.3 %copy-start.7 = (s32[1024]{0:T(1024)S(1)}, s32[1024]{0:T(1024)}, u32[]{:S(2)}) copy-start(s32[1024]{0:T(1024)} %param.20) | copy-start | bytes 12292
  0.7 28.3 %copy-start.8 = (s32[1024]{0:T(1024)S(1)}, s32[1024]{0:T(1024)}, u32[]{:S(2)}) copy-start(s32[1024]{0:T(1024)} %param.21) | copy-start | bytes 12292
  0.7 28.3 %copy-start.9 = (f32[512]{0:T(512)S(1)}, f32[512]{0:T(512)}, u32[]{:S(2)}) copy-start(f32[512]{0:T(512)} %param.24) | copy-start | bytes 6148
  0.7 28.3 %copy-start.10 = (f32[512]{0:T(512)S(1)}, f32[512]{0:T(512)}, u32[]{:S(2)}) copy-start(f32[512]{0:T(512)} %param.27) | copy-start | bytes 6148

commit v3 on v2

--- a/solution.py
+++ b/solution.py
@@ -64,10 +64,12 @@
     edge_in_ref,
     edge_out_ref,
     gain_ref,
+    coarse_ref,
+    coarse_to_ref,
     fine_next_ref,
     total_ref,
     every_ref,
-    recv_table_ref,
+    coarse_base_ref,
     node,
     thirds,
     edge_out,
@@ -78,6 +80,9 @@
     rims,
     edge_half,
     edge_buf,
+    base,
+    coarse_buf,
+    coarse_to,
     sender_ids,
     receiver_ids,
     edge_sem,
@@ -130,6 +135,8 @@
                 (receiver_ref, receiver),
                 (edge_out_ref, edge_out),
                 (gain_ref, gain),
+                (coarse_ref, coarse_buf),
+                (coarse_to_ref, coarse_to),
             )
         )
     ]
@@ -144,10 +151,12 @@
         pl.semaphore_signal(
             barrier, inc=1, device_id={"lon": other_lon, "lat": other_lat}, device_id_type=MESH
         )
-    for load in loads[2:]:
+    for load in loads[2:8]:
         load.start()
     for t in range(tiles):
         edge_copy(t).start()
+    for load in loads[8:]:
+        load.start()
     for load in loads[:2]:
         load.wait()
 
@@ -233,20 +242,20 @@
         passed[k].start()
 
     pl.semaphore_wait(barrier, len(partners))
+    own[0].start()
     for copy in halos:
         copy.start()
-    for copy in own:
+    for copy in own[1:]:
         copy.start()
     keep = pltpu.make_async_copy(table.at[pl.ds(0, GROUP)], block(lon, lat), own_sem)
     keep.start()
 
-    for load in loads[2:]:
+    for load in loads[2:8]:
         load.wait()
     receivers = (matmul(node[...], thirds[pl.ds(2 * width, width), :]) * 0.5).astype(
         jnp.bfloat16
     )
     table[pl.ds(recv_base, nodes), :] = receivers
-    recv_table_ref[...] = receivers
     edge_half[...] = thirds[pl.ds(0, width), :] * jnp.bfloat16(0.5)
     total_ref[...] = jnp.zeros_like(total_ref)
 
@@ -268,32 +277,37 @@
     sender_ids[...] = local.astype(jnp.float32)
     receiver_ids[...] = receiver[...].astype(jnp.float32)
 
+    groups = TILE // GROUP
+    per_sub = SUB // GROUP
+
+    def base_tile(t, carry):
+        edge_copy(t).wait()
+        rows = pl.ds(pl.multiple_of(t * TILE, TILE), TILE)
+        tos = [receiver_ids[pl.ds(t * groups + g, 1), :] for g in range(groups)]
+        base[rows, :] = matmul(edge_buf[rows, :], edge_half[...]) + matmul(
+            one_hot(tos, nodes), table[pl.ds(recv_base, nodes), :]
+        )
+        return carry
+
+    lax.fori_loop(0, tiles, base_tile, 0)
     for copy in halos:
         copy.wait_recv()
-
-    groups = TILE // GROUP
-    per_sub = SUB // GROUP
 
     def tile(t, carry):
         @pl.when(t == 1)
         def _():
             from_band(1)
-
-        @pl.when(t == 2)
+            from_across(0)
+
+        @pl.when(t == 3)
         def _():
             from_band(2)
-            from_across(0)
-
-        @pl.when(t == 3)
+
+        @pl.when(t == 5)
         def _():
             from_band(3)
             from_across(1)
 
-        @pl.when(t == 5)
-        def _():
-            from_across(2)
-
-        edge_copy(t).wait()
         to_rows, messages = [], []
         for part in range(TILE // SUB):
             first = t * TILE + part * SUB
@@ -303,9 +317,10 @@
                 receiver_ids[pl.ds(t * groups + part * per_sub + g, 1), :] for g in range(per_sub)
             ]
             to_rows += tos
-            picks = jnp.concatenate([one_hot(ids, nodes + HALO), one_hot(tos, nodes)], axis=1)
             edges = edge_buf[rows, :]
-            half = matmul(edges, edge_half[...]) + matmul(picks, table[...])
+            half = base[rows, :] + matmul(
+                one_hot(ids, nodes + HALO), table[pl.ds(0, nodes + HALO), :]
+            )
             change = normed(matmul(silu_of_twice(half), edge_out[...]), gain[...])
             fine_next_ref[rows, :] = (edges.astype(jnp.float32) + change).astype(jnp.bfloat16)
             messages.append(change.astype(jnp.bfloat16))
@@ -314,6 +329,17 @@
         return carry
 
     lax.fori_loop(0, tiles, tile, 0)
+    from_across(2)
+    for load in loads[8:]:
+        load.wait()
+    coarse_tos = coarse_to[...].astype(jnp.float32)
+    for part in range(coarse_buf.shape[0] // LAST):
+        rows = pl.ds(part * LAST, LAST)
+        first = part * (LAST // GROUP)
+        tos = [coarse_tos[first + g : first + g + 1, :] for g in range(LAST // GROUP)]
+        coarse_base_ref[rows, :] = matmul(coarse_buf[rows, :], edge_half[...]) + matmul(
+            one_hot(tos, nodes), table[pl.ds(recv_base, nodes), :]
+        )
     from_across(3)
     for band in bands:
         arrived(twin, band)
@@ -330,9 +356,8 @@
     row_ref,
     receiver_ref,
     every_ref,
-    recv_table_ref,
+    coarse_base_ref,
     total_ref,
-    edge_in_ref,
     edge_out_ref,
     gain_ref,
     node_ref,
@@ -359,10 +384,8 @@
         tos = [to[part * per + g : part * per + g + 1, :] for g in range(per)]
         rows = pl.ds(part * LAST, LAST)
         edges = coarse_ref[rows, :]
-        half = (
-            matmul(edges, edge_in_ref[pl.ds(0, width), :]) * 0.5
-            + matmul(one_hot(ids, every_ref.shape[0]), every_ref[...])
-            + matmul(one_hot(tos, nodes), recv_table_ref[...])
+        half = coarse_base_ref[rows, :] + matmul(
+            one_hot(ids, every_ref.shape[0]), every_ref[...]
         )
         change = normed(matmul(silu_of_twice(half), edge_out_ref[...]), gain_ref[...])
         coarse_buf[rows, :] = (edges.astype(jnp.float32) + change).astype(jnp.bfloat16)
@@ -407,15 +430,15 @@
     hbm = pl.BlockSpec(memory_space=pltpu.HBM)
     table_rows = 2 * nodes + HALO
     dma = pltpu.SemaphoreType.DMA
-    fine_made, total, every, recv_table = pl.pallas_call(
+    fine_made, total, every, coarse_base = pl.pallas_call(
         fine_kernel,
         out_shape=(
             jax.ShapeDtypeStruct((fine, width), jnp.bfloat16),
             jax.ShapeDtypeStruct((nodes, width), jnp.float32),
             jax.ShapeDtypeStruct((everyone, width), jnp.bfloat16),
-            jax.ShapeDtypeStruct((nodes, width), jnp.bfloat16),
+            jax.ShapeDtypeStruct((coarse, width), jnp.float32),
         ),
-        in_specs=[hbm] * 7,
+        in_specs=[hbm] * 9,
         out_specs=(vmem,) * 4,
         scratch_shapes=[
             pltpu.VMEM((nodes, width), jnp.bfloat16),
@@ -428,10 +451,13 @@
             pltpu.VMEM((2 * RIM_LAT, width), jnp.bfloat16),
             pltpu.VMEM((width, width), jnp.bfloat16),
             pltpu.VMEM((fine, width), jnp.bfloat16),
+            pltpu.VMEM((fine, width), jnp.float32),
+            pltpu.VMEM((coarse, width), jnp.bfloat16),
+            pltpu.VMEM((coarse // GROUP, GROUP), jnp.int32),
             pltpu.VMEM((fine // GROUP, GROUP), jnp.float32),
             pltpu.VMEM((fine // GROUP, GROUP), jnp.float32),
             dma((tiles,)),
-            dma((8,)),
+            dma((10,)),
             dma,
             dma((8,)),
             dma((8,)),
@@ -455,6 +481,8 @@
                 edge_in,
                 edge_out,
                 edge_gain.reshape(1, width),
+                coarse_edges,
+                coarse_receiver.reshape(coarse // GROUP, GROUP),
             )
         ]
     )
@@ -465,7 +493,7 @@
             jax.ShapeDtypeStruct((coarse, width), jnp.bfloat16),
             jax.ShapeDtypeStruct((nodes, width), jnp.bfloat16),
         ),
-        in_specs=[vmem] * 15,
+        in_specs=[vmem] * 14,
         out_specs=(hbm, hbm, vmem),
         scratch_shapes=[
             pltpu.VMEM((coarse, width), jnp.bfloat16),
@@ -482,9 +510,8 @@
         coarse_row.reshape(coarse // GROUP, GROUP),
         coarse_receiver.reshape(coarse // GROUP, GROUP),
         every,
-        recv_table,
+        coarse_base,
         total,
-        edge_in,
         edge_out,
         edge_gain.reshape(1, width),
         node_latent,

time: 36.4 us -> 33.9 us (0.931)
  Pallas kernels: 35.4 us -> 33 us
    pallas_call x1, Pallas kernels: 28.2 us -> 26.8 us  [fast_shards(): pl.pallas_call(fine_kernel, out_shape=(jax.ShapeDtypeStruct((fine, width)...]
    pallas_call x1, Pallas kernels: 7.24 us -> 6.15 us  [fast_shards(): pl.pallas_call(last_kernel, out_shape=(jax.ShapeDtypeStruct((fine, width)...]
where the time goes in v3:
time: 33.9 us; the launch traced here: 33.8 us
  Pallas kernels  33 us (97%)
  between operations  0.8 us (2%)
    pallas_call x1, Pallas kernels, fast_shards(): pl.pallas_call(fine_kernel, out_shape=(jax.ShapeDtypeStruct((fine, width)...  26.8 us
    pallas_call x1, Pallas kernels, fast_shards(): pl.pallas_call(last_kernel, out_shape=(jax.ShapeDtypeStruct((fine, width)...  6.15 us

profile of v3, /device:TPU:0, one launch (start us, length us, event | category | flops | bytes accessed | tf_op | source)
XLA Modules:
  0.0 33.8 jit_solution(1575981903705861961)
XLA Ops:
  0.6 0.0 copy-start
  0.6 0.0 copy-start.1
  0.7 0.0 copy-start.2
  0.7 0.0 copy-start.3
  0.7 0.0 copy-start.4
  0.7 0.0 copy-start.5
  0.7 0.0 copy-start.6
  0.7 0.0 copy-start.7
  0.7 0.0 copy-start.8
  0.7 0.0 copy-start.9
  0.7 26.8 %shard_map.157 = (bf16[3072,512]{1,0:T(8,128)(2,1)S(1)}, f32[512,512]{1,0:T(8,128)S(1)}, bf16[2048,512]{1,0:T(8,128)(2,1)S(1)}, f32[1024,512]{1,0:T(8,128)S(1)}) custom-call(bf16[512,512]{1,0:T(8,128)(2,1)} %node_ref.3, bf16[3072,512]{1,0:T(8,128)(2,1)} %edges_ref.1, s32[24,128]{1,0:T(8,128)} %bitcast.14, s32[24,128]{1,0:T(8,128)} %bitcast.15, ...), custom_call_target="tpu_custom_call" | custom-call | flops 10000000000 | bytes 12582912 | tf_op jit(solution)/shard_map/pallas_call | solution.py:433
  27.6 0.0 copy-done
  27.6 0.0 copy-done.1
  27.6 0.0 copy-done.2
  27.6 0.0 copy-done.3
  27.6 0.0 copy-done.4
  27.6 0.0 copy-done.5
  27.6 0.0 copy-done.6
  27.6 0.0 copy-done.7
  27.6 0.0 copy-done.8
  27.6 0.0 copy-done.9
  27.7 6.1 %shard_map.158 = (bf16[3072,512]{1,0:T(8,128)(2,1)}, bf16[1024,512]{1,0:T(8,128)(2,1)}, bf16[512,512]{1,0:T(8,128)(2,1)}) custom-call(bf16[3072,512]{1,0:T(8,128)(2,1)S(1)} %get-tuple-element.10.fine_ref, bf16[1024,512]{1,0:T(8,128)(2,1)S(1)} %copy-done, s32[8,128]{1,0:T(8,128)S(1)} %bitcast.9, s32[8,128]{1,0:T(8,128)S(1)} %bitcast.10, ...), custom_call_target="tpu_custom_call" | custom-call | flops 5000000000 | bytes 16777216 | tf_op jit(solution)/shard_map/pallas_call | solution.py:489
Async XLA Ops:
  0.6 26.9 %copy-start = (bf16[1024,512]{1,0:T(8,128)(2,1)S(1)}, bf16[1024,512]{1,0:T(8,128)(2,1)}, u32[]{:S(2)}) copy-start(bf16[1024,512]{1,0:T(8,128)(2,1)} %coarse_ref.3) | copy-start | bytes 3145732
  0.6 26.9 %copy-start.1 = (bf16[1024,512]{1,0:T(8,128)(2,1)S(1)}, bf16[1024,512]{1,0:T(8,128)(2,1)}, u32[]{:S(2)}) copy-start(bf16[1024,512]{1,0:T(8,128)(2,1)} %node_in_ref.1) | copy-start | bytes 3145732
  0.7 26.9 %copy-start.2 = (bf16[512,512]{1,0:T(8,128)(2,1)S(1)}, bf16[512,512]{1,0:T(8,128)(2,1)}, u32[]{:S(2)}) copy-start(bf16[512,512]{1,0:T(8,128)(2,1)} %node_ref.3) | copy-start | bytes 1572868
  0.7 26.9 %copy-start.3 = (bf16[512,512]{1,0:T(8,128)(2,1)S(1)}, bf16[512,512]{1,0:T(8,128)(2,1)}, u32[]{:S(2)}) copy-start(bf16[512,512]{1,0:T(8,128)(2,1)} %edge_out_ref.3) | copy-start | bytes 1572868
  0.7 26.9 %copy-start.4 = (bf16[512,512]{1,0:T(8,128)(2,1)S(1)}, bf16[512,512]{1,0:T(8,128)(2,1)}, u32[]{:S(2)}) copy-start(bf16[512,512]{1,0:T(8,128)(2,1)} %node_out_ref.1) | copy-start | bytes 1572868
  0.7 26.9 %copy-start.5 = (s32[1024]{0:T(1024)S(1)}, s32[1024]{0:T(1024)}, u32[]{:S(2)}) copy-start(s32[1024]{0:T(1024)} %param.21) | copy-start | bytes 12292
  0.7 26.9 %copy-start.6 = (s32[1024,1]{0,1:T(1,128)S(1)}, s32[1024,1]{0,1:T(1,128)}, u32[]{:S(2)}) copy-start(s32[1024,1]{0,1:T(1,128)} %param.19) | copy-start | bytes 12292
  0.7 26.9 %copy-start.7 = (s32[1024]{0:T(1024)S(1)}, s32[1024]{0:T(1024)}, u32[]{:S(2)}) copy-start(s32[1024]{0:T(1024)} %param.20) | copy-start | bytes 12292
  0.7 26.9 %copy-start.8 = (f32[512]{0:T(512)S(1)}, f32[512]{0:T(512)}, u32[]{:S(2)}) copy-start(f32[512]{0:T(512)} %param.24) | copy-start | bytes 6148
  0.7 26.9 %copy-start.9 = (f32[512]{0:T(512)S(1)}, f32[512]{0:T(512)}, u32[]{:S(2)}) copy-start(f32[512]{0:T(512)} %param.27) | copy-start | bytes 6148
